TPU v7x, 32 devices: a whole 2x2x4 slice. The times are simulated.
32 devices in a mesh: tbl: 16 (over z, y, x), row: 2 (over core).
Axes of the slice: x: 2, y: 2, z: 4, core: 2. Of those that a mesh axis runs over, the one named last changes fastest.
Arguments:
- slab: bfloat16 [2048, 256], P(('tbl', 'row')), may hold values from -1.1953125 to 1.1953125
- counts: int32 [4096, 2048], P(None, ('tbl', 'row')), may hold values 0 or 1
- cross_down: bfloat16 [4096, 512], replicated, may hold values from -0.09375 to 0.09375
- cross_up: bfloat16 [512, 4096], replicated, may hold values from -0.25 to 0.25
- cross_bias: float32 [4096], replicated, may hold values from -3 to 3
- out_weight: float32 [4096], replicated, may hold values from -0.09375 to 0.09375
- labels: int32 [4096], P(('tbl', 'row')), may hold values 0 or 1
Outputs:
- grad_slab: float32 [2048, 256], P(('tbl', 'row'))
- grad_down: bfloat16 [4096, 512], P(('tbl', 'row'))
- grad_up: bfloat16 [512, 4096], P(None, ('tbl', 'row'))
- grad_bias: float32 [4096], P(('tbl', 'row'))
- grad_out: float32 [4096], P(('tbl', 'row'))
All inputs are finite; a program needn't handle non-finite values. No bound on the sum of `counts` or of `labels` on one device may be relied on, other than what follows from the above.
Results may differ from a plain program's by a relative error of at most 0.022.
Values may be sent and summed in bfloat16 or wider, within the bound.
A program may use at most 128 MiB of HBM per device.

v0:
```python
import jax
import jax.numpy as jnp
from jax import lax
from jax.sharding import PartitionSpec as P

TABLES = 16


def local(slab, counts, cross_down, cross_up, cross_bias, out_weight, labels):
    tbl_count = lax.axis_size("tbl")
    row_count = lax.axis_size("row")
    device_count = tbl_count * row_count
    row_width = slab.shape[1]
    rows_local = slab.shape[0]
    batch_all = counts.shape[0]
    samples_local = batch_all // device_count
    per_group = TABLES // tbl_count
    group_width = per_group * row_width
    counts_half = counts.astype(jnp.bfloat16)
    grouped = counts_half.reshape(tbl_count, row_count * samples_local, rows_local)
    chosen = grouped
    partial_value = jnp.einsum("tbr,re->bte", chosen, slab, preferred_element_type=jnp.float32)
    shares = lax.psum_scatter(
        partial_value.astype(jnp.bfloat16), "row", scatter_dimension=0, tiled=True
    )
    owned = lax.all_to_all(shares, "tbl", split_axis=1, concat_axis=2, tiled=True)
    pooled = owned.reshape(samples_local, tbl_count * group_width)
    cross_width = pooled.shape[1]
    pooled_full = pooled.astype(jnp.float32)
    squeezed = jnp.dot(pooled, cross_down, preferred_element_type=jnp.float32).astype(jnp.bfloat16)
    cross_gain = jnp.dot(squeezed, cross_up, preferred_element_type=jnp.float32) + cross_bias
    crossed = pooled_full * cross_gain + pooled_full
    logits = jnp.sum(crossed * out_weight, axis=1)
    grad_logits = jax.nn.sigmoid(logits) - labels.astype(jnp.float32)
    grad_out = jnp.sum(crossed * grad_logits[:, None], axis=0)
    grad_crossed = grad_logits[:, None] * out_weight
    grad_gain = grad_crossed * pooled_full
    grad_bias = jnp.sum(grad_gain, axis=0)
    gain_half = grad_gain.astype(jnp.bfloat16)
    grad_squeezed = jnp.einsum(
        "bd,rd->br", gain_half, cross_up, preferred_element_type=jnp.float32
    ).astype(jnp.bfloat16)
    grad_pooled = (
        grad_crossed * (cross_gain + 1.0)
        + jnp.einsum("br,dr->bd", grad_squeezed, cross_down, preferred_element_type=jnp.float32)
    ).astype(jnp.bfloat16)
    column_count = cross_width // device_count
    pooled_cols, gain_cols = (
        lax.all_to_all(
            pooled.reshape(samples_local, device_count, column_count),
            ("tbl", "row"),
            split_axis=1,
            concat_axis=0,
            tiled=True,
        ),
        lax.all_to_all(
            gain_half.reshape(samples_local, device_count, column_count),
            ("tbl", "row"),
            split_axis=1,
            concat_axis=0,
            tiled=True,
        ),
    )
    pooled_cols = pooled_cols.reshape(batch_all, column_count)
    gain_cols = gain_cols.reshape(batch_all, column_count)
    down_total = jnp.einsum(
        "bd,br->dr",
        pooled_cols,
        lax.all_gather(grad_squeezed, ("tbl", "row"), axis=0, tiled=True),
        preferred_element_type=jnp.float32,
    )
    up_total = jnp.einsum(
        "br,bd->rd",
        lax.all_gather(squeezed, ("tbl", "row"), axis=0, tiled=True),
        gain_cols,
        preferred_element_type=jnp.float32,
    )
    sum_bias, sum_out = (
        lax.psum_scatter(grad_bias, ("tbl", "row"), scatter_dimension=0, tiled=True),
        lax.psum_scatter(grad_out, ("tbl", "row"), scatter_dimension=0, tiled=True),
    )
    returned = lax.all_to_all(
        grad_pooled.reshape(samples_local, 1, tbl_count * group_width),
        "tbl",
        split_axis=2,
        concat_axis=1,
        tiled=True,
    )
    chosen = grouped
    columns = lax.all_gather(returned, "row", axis=0, tiled=True)
    grad_slab = jnp.einsum("tbr,bte->re", chosen, columns, preferred_element_type=jnp.float32)
    return (
        grad_slab,
        down_total.astype(jnp.bfloat16),
        up_total.astype(jnp.bfloat16),
        sum_bias,
        sum_out,
    )


def solution(mesh):
    placed = (
        P(("tbl", "row"), None),
        P(None, ("tbl", "row")),
        P(),
        P(),
        P(),
        P(),
        P(("tbl", "row")),
    )
    return jax.shard_map(
        local,
        mesh=mesh,
        in_specs=placed,
        out_specs=(
            P(("tbl", "row"), None),
            P(("tbl", "row"), None),
            P(None, ("tbl", "row")),
            P(("tbl", "row")),
            P(("tbl", "row")),
        ),
        check_vma=False,
    )
```

profile of v0, /device:TPU:25, one launch (start us, length us, event | category | flops | bytes accessed | tf_op | source)
XLA Modules:
  0.0 303.2 jit_solution(17561152967648962213)
XLA Ops:
  7.2 1.3 convert_element_type.42
  8.5 0.7 convolution_convert_fusion
  9.3 3.0 copy.36
  12.3 11.4 %reduce-scatter.4.cloned.1.call-done = bf16[128,4096]{1,0:T(8,128)(2,1)} async-done(((bf16[256,4096]{1,0:T(8,128)(2,1)}), bf16[128,4096]{1,0:T(8,128)(2,1)}) %reduce-scatter.4.cloned.1.call-update) | async-done | bytes 1048592
  23.7 1.6 copy.37
  25.3 30.1 %all_to_all.51 = bf16[128,16,256]{0,2,1:T(8,128)(2,1)} all-to-all(bf16[128,16,256]{0,2,1:T(8,128)(2,1)S(1)} %bitcast.54), channel_id=1, replica_groups=mesh['tbl'=16,'row'=2] {'tbl'}, dimensions={1} | all-to-all | bytes 2097152 | tf_op jit(solution)/shard_map/all_to_all | solution.py:26
  55.5 1.5 copy.33
  57.0 3.3 %convolution_convert_fusion.4 = bf16[128,512]{1,0:T(8,128)(2,1)S(1)} fusion(bf16[128,4096]{0,1:T(8,128)(2,1)} %bitcast.2, bf16[4096,512]{1,0:T(8,128)(2,1)} %param.9), kind=kOutput, calls=%fused_computation.16 | convolution fusion | flops 536936448 | bytes 5373952 | tf_op jit(solution)/shard_map/dot_general | solution.py:30
  60.3 3.6 %multiply_reduce_fusion.2 = (f32[128]{0:T(128)S(1)}, f32[128,4096]{1,0:T(8,128)S(1)}) fusion(bf16[128,4096]{1,0:T(8,128)(2,1)S(1)} %copy.33, f32[4096]{0:T(1024)S(1)} %copy-done.6, f32[4096]{0:T(1024)S(1)} %copy-done.7, bf16[128,512]{1,0:T(8,128)(2,1)S(1)} %convolution_convert_fusion.4, bf16[512,4096]{1,0:T(8,128)(2,1)} %param.10), kind=kOutput, calls=%fused_computation.11 | convolution fusion | flops 540016512 | bytes 7504384 | tf_op jit(solution)/shard_map/dot_general | solution.py:31
  63.9 1.5 convolution_convert_fusion.3
  65.5 4.7 %fusion.1 = bf16[128,1,4096]{2,0,1:T(8,128)(2,1)} fusion(bf16[128,512]{1,0:T(8,128)(2,1)S(1)} %convolution_convert_fusion.3, bf16[4096,512]{1,0:T(8,128)(2,1)} %param.9, f32[128,4096]{1,0:T(8,128)S(1)} %get-tuple-element.8, f32[128]{0:T(128)S(1)} %divide_subtract_fusion, f32[4096]{0:T(1024)S(1)} %copy-done.6), kind=kOutput, calls=%fused_computation.3 | convolution fusion | flops 539492352 | bytes 7488000 | tf_op jit(solution)/shard_map/br,dr->bd/dot_general | solution.py:45
  70.2 5.5 %copy.28 = bf16[128,1,4096]{0,1,2:T(2,128)(2,1)} copy(bf16[128,1,4096]{2,0,1:T(8,128)(2,1)} %fusion.1) | data formatting | bytes 2097152 | tf_op jit(solution)/shard_map/reshape | solution.py:83
  76.2 24.4 %reduce.1 = bf16[4096,128]{1,0:T(8,128)(2,1)} reduce(bf16[4096,1,128]{2,1,0:T(2,128)(2,1)} %bitcast.49, bf16[]{:T(256)} %broadcast.22), dimensions={1}, to_apply=%bitcast.34.reduce_sub_computation | reduce | bytes 2097154
  100.7 2.1 reshape.67
  102.8 29.2 %all_to_all.52 = bf16[16,2,16384]{2,1,0:T(2,128)(2,1)} all-to-all(bf16[16,2,16384]{2,1,0:T(2,128)(2,1)} %reshape.67), channel_id=1, replica_groups=mesh['tbl'=16,'row'=2] {'tbl'}, dimensions={0} | all-to-all | bytes 2097152 | tf_op jit(solution)/shard_map/all_to_all | solution.py:82
  132.0 5.8 %reshape.68 = bf16[4096,1,128]{2,1,0:T(2,128)(2,1)} reshape(bf16[16,2,16384]{2,1,0:T(2,128)(2,1)} %all_to_all.52) | data formatting | bytes 2097152
  137.8 2.7 copy.38
  140.5 2.3 copy.29
  142.8 0.7 all-gather.6.cloned.1.call-update
  144.1 7.1 %all-to-all-start.2 = ((bf16[128,32,128]{0,2,1:T(8,128)(2,1)}), bf16[128,32,128]{0,2,1:T(8,128)(2,1)}, u32[]{:S(2)}, u32[]{:S(2)}) async-start(bf16[128,32,128]{0,2,1:T(8,128)(2,1)} %bitcast.6), calls=%async_computation.2 | async-start | bytes 2097152 | tf_op jit(solution)/shard_map/all_to_all | solution.py:49
  151.2 2.6 multiply_convert_fusion
  153.8 22.7 %all-to-all-done.2 = bf16[128,32,128]{0,2,1:T(8,128)(2,1)} async-done(((bf16[128,32,128]{0,2,1:T(8,128)(2,1)}), bf16[128,32,128]{0,2,1:T(8,128)(2,1)}, u32[]{:S(2)}, u32[]{:S(2)}) %all-to-all-start.2) | async-done | bytes 1048608 | tf_op jit(solution)/shard_map/all_to_all | solution.py:49
  176.5 6.5 %all-to-all-start.3 = ((bf16[128,32,128]{0,2,1:T(8,128)(2,1)}), bf16[128,32,128]{0,2,1:T(8,128)(2,1)}, u32[]{:S(2)}, u32[]{:S(2)}) async-start(bf16[128,32,128]{0,2,1:T(8,128)(2,1)} %multiply_convert_fusion), calls=%async_computation.3 | async-start | bytes 2097152 | tf_op jit(solution)/shard_map/all_to_all | solution.py:56
  183.0 2.3 multiply_reduce_fusion.1
  185.8 50.5 %all-reduce.2 = (f32[4096]{0:T(1024)S(1)}, f32[4096]{0:T(1024)S(1)}) all-reduce(f32[4096]{0:T(1024)S(1)} %bitcast.59, f32[4096]{0:T(1024)S(1)} %multiply_reduce_fusion), channel_id=3, replica_groups=mesh['tbl'=16,'row'=2] {'tbl','row'}, use_global_device_ids=true, to_apply=%region_3.0.clone | all-reduce | flops 8192 | bytes 65536
  236.3 0.6 dynamic-slice
  237.4 1.7 copy.31
  239.1 1.6 copy.32
  240.8 2.7 convolution_bitcast_fusion
  243.5 3.6 %convolution_convert_fusion.2 = bf16[128,512]{1,0:T(8,128)(2,1)} fusion(bf16[4096,128]{1,0:T(8,128)(2,1)S(1)} %bitcast.55, bf16[4096,512]{1,0:T(8,128)(2,1)} %all-gather.6.cloned.1.call-done), kind=kOutput, calls=%fused_computation.14 | convolution fusion | flops 536936448 | bytes 5373952 | tf_op jit(solution)/shard_map/bd,br->dr/dot_general | solution.py:66
  247.1 45.4 %all-gather.8.cloned.1.call-done = bf16[4096,512]{1,0:T(8,128)(2,1)} async-done(((bf16[128,512]{1,0:T(8,128)(2,1)}), bf16[4096,512]{1,0:T(8,128)(2,1)}) %all-gather.8.cloned.1.call-update) | async-done | bytes 4194320 | tf_op jit(solution)/shard_map/all_gather | solution.py:74
  292.6 4.1 %convolution_convert_fusion.1 = bf16[512,128]{1,0:T(8,128)(2,1)} fusion(bf16[4096,512]{1,0:T(8,128)(2,1)} %all-gather.8.cloned.1.call-done, bf16[4096,128]{1,0:T(8,128)(2,1)S(1)} %bitcast.56), kind=kOutput, calls=%fused_computation.13 | convolution fusion | flops 536936448 | bytes 5373952 | tf_op jit(solution)/shard_map/br,bd->rd/dot_general | solution.py:72
  (34 shorter events, 2.3 us)
Async XLA Ops:
  7.2 1.4 copy-start
  7.2 16.5 %reduce-scatter.4.cloned.1.call-start = ((), (), s32[]{:S(2)}) async-start(), calls=%async_computation.8 | async-start | bytes 3145728
  8.5 3.7 %copy-start.2 = (bf16[4096,64]{0,1:T(8,128)(2,1)}, bf16[4096,64]{0,1:T(8,128)(2,1)S(1)}, u32[]{:S(2)}) copy-start(bf16[4096,64]{0,1:T(8,128)(2,1)S(1)} %convert_element_type.42) | copy-start | bytes 1572868
  12.3 228.5 %all-gather.4.cloned.1.call-start = ((), (), s32[]{:S(2)}) async-start(), calls=%async_computation.5 | async-start | bytes 3145728 | tf_op jit(solution)/shard_map/all_gather | solution.py:90
  56.9 3.3 %copy-start.6 = (f32[4096]{0:T(1024)S(1)}, f32[4096]{0:T(1024)}, u32[]{:S(2)}) copy-start(f32[4096]{0:T(1024)} %param.12) | copy-start | bytes 49156
  57.0 3.3 %copy-start.7 = (f32[4096]{0:T(1024)S(1)}, f32[4096]{0:T(1024)}, u32[]{:S(2)}) copy-start(f32[4096]{0:T(1024)} %param.11) | copy-start | bytes 49156
  60.2 3.6 %copy-start.4 = (bf16[128,512]{1,0:T(8,128)(2,1)}, bf16[128,512]{1,0:T(8,128)(2,1)S(1)}, u32[]{:S(2)}) copy-start(bf16[128,512]{1,0:T(8,128)(2,1)S(1)} %convolution_convert_fusion.4) | copy-start | bytes 393220
  60.3 3.6 %copy-start.8 = (s32[128]{0:T(128)S(1)}, s32[128]{0:T(128)}, u32[]{:S(2)}) copy-start(s32[128]{0:T(128)} %param.13) | copy-start | bytes 1540
  60.3 3.6 %copy-start.1 = (bf16[512,4096]{1,0:T(8,128)(2,1)S(1)}, bf16[512,4096]{1,0:T(8,128)(2,1)}, u32[]{:S(2)}) copy-start(bf16[512,4096]{1,0:T(8,128)(2,1)} %param.10) | copy-start | bytes 12582916
  65.5 4.7 %copy-start.5 = (bf16[128,512]{1,0:T(8,128)(2,1)}, bf16[128,512]{1,0:T(8,128)(2,1)S(1)}, u32[]{:S(2)}) copy-start(bf16[128,512]{1,0:T(8,128)(2,1)S(1)} %convolution_convert_fusion.3) | copy-start | bytes 393220
  142.8 100.8 %all-gather.6.cloned.1.call-start = ((), (), s32[]{:S(2)}) async-start(), calls=%async_computation.6 | async-start | bytes 4325376 | tf_op jit(solution)/shard_map/all_gather | solution.py:69
  143.5 149.1 %all-gather.8.cloned.1.call-start = ((), (), s32[]{:S(2)}) async-start(), calls=%async_computation.7 | async-start | bytes 4325376 | tf_op jit(solution)/shard_map/all_gather | solution.py:74
  144.1 32.4 %all-to-all-start.2 = ((bf16[128,32,128]{0,2,1:T(8,128)(2,1)}), bf16[128,32,128]{0,2,1:T(8,128)(2,1)}, u32[]{:S(2)}, u32[]{:S(2)}) async-start(bf16[128,32,128]{0,2,1:T(8,128)(2,1)} %bitcast.6), calls=%async_computation.2 | async-start | bytes 2097152 | tf_op jit(solution)/shard_map/all_to_all | solution.py:49
  176.5 62.7 %all-to-all-start.3 = ((bf16[128,32,128]{0,2,1:T(8,128)(2,1)}), bf16[128,32,128]{0,2,1:T(8,128)(2,1)}, u32[]{:S(2)}, u32[]{:S(2)}) async-start(bf16[128,32,128]{0,2,1:T(8,128)(2,1)} %multiply_convert_fusion), calls=%async_computation.3 | async-start | bytes 2097152 | tf_op jit(solution)/shard_map/all_to_all | solution.py:56
  237.4 3.4 %copy-start.3 = (bf16[4096,64]{0,1:T(8,128)(2,1)S(1)}, bf16[4096,64]{0,1:T(8,128)(2,1)}, u32[]{:S(2)}) copy-start(bf16[4096,64]{0,1:T(8,128)(2,1)} %copy-done.2) | copy-start | bytes 1572868
Sparse Core Ops, SparseCore 0:
  12.4 11.2 reduce-scatter.3
  142.9 12.6 all-gather.3
  159.4 69.2 all-gather.5
  231.8 60.6 all-gather.7
where the time goes:
time: 307 us; the launch traced here: 303 us
  blocking collectives  110 us (36%)
  waiting for transfers between devices  80.8 us (26%)
  other arithmetic  31 us (10%)
  local copies, waits for them, and re-layouts  29.5 us (10%)
  matrix products  24.3 us (8%)
  between operations  14 us (5%)
  starting transfers between devices  13.8 us (4%)
    unnamed x1, blocking collectives  50.5 us
    all_gather x1, waiting for transfers between devices, local(): lax.all_gather(squeezed, ('tbl', 'row'), axis=0, tiled=True)  45.4 us
    all_to_all x1, blocking collectives, local(): lax.all_to_all(shares, 'tbl', split_axis=1, concat_axis=2, tiled=True)  30.1 us
    all_to_all x1, blocking collectives, local(): lax.all_to_all(grad_pooled.reshape(samples_local, 1, tbl_count * group_wi...  29.2 us
    unnamed x1, other arithmetic  24.4 us
    all_to_all x1, waiting for transfers between devices, local(): lax.all_to_all(pooled.reshape(samples_local, device_count, column_count),...  22.7 us
    unnamed x27, local copies, waits for them, and re-layouts  16.9 us
    unnamed x5, waiting for transfers between devices  12.6 us
  transfers between devices with their start and end apart: 6, of which 3 were waited for; matrix products, arithmetic and copies ran while one was open for 5% of the time, Pallas kernels for 0%

commit v1 on v0

v1 whole, which is shorter than its diff:
```python
import functools
import math

import jax
import jax.numpy as jnp
from jax import lax
from jax.sharding import Mesh, PartitionSpec as P


def inner_count(count):
    width = max(1, math.isqrt(count))
    while count % width:
        width -= 1
    return width


def local(slab, counts, cross_down, cross_up, cross_bias, out_weight, labels):
    z_count, q_count, row_count = (lax.axis_size(name) for name in ("z", "q", "row"))
    table_count = z_count * q_count
    rows_local, embed = slab.shape
    samples = labels.shape[0]
    rank = cross_down.shape[1]
    half, full = jnp.bfloat16, jnp.float32
    dot = functools.partial(jnp.einsum, preferred_element_type=full)
    my_table = lax.axis_index("z") * q_count + lax.axis_index("q")
    flipped = counts.T.astype(half).reshape(rows_local, z_count, q_count, row_count, samples)
    flipped = flipped.transpose(1, 3, 0, 2, 4).reshape(z_count * row_count, rows_local, q_count * samples)
    mine = lax.all_to_all(flipped, ("z", "row"), 0, 0, tiled=True)
    mine = mine.reshape(z_count * row_count * rows_local, q_count, samples)
    own = lax.all_to_all(mine, "q", 1, 0, tiled=True)
    own = own.reshape(q_count, z_count, row_count * rows_local, samples).swapaxes(0, 1)
    tables = lax.all_gather(slab, ("z", "q", "row"), axis=0, tiled=True)
    tables = tables.reshape(table_count, row_count * rows_local, embed)
    weighted = (tables.astype(full) * out_weight.reshape(table_count, 1, embed)).astype(half)
    down = cross_down.reshape(table_count, embed, rank)
    up = cross_up.reshape(rank, table_count, embed)
    factors = jnp.concatenate(
        [dot("tpe,ter->tpr", tables, down), dot("tpe,rte->tpr", weighted, up)], axis=2
    ).astype(half)
    head = ((1.0 + cross_bias) * out_weight).reshape(table_count, 1, embed)
    direct = jnp.sum(tables.astype(full) * head, axis=2)
    own = own.reshape(table_count * row_count * rows_local, samples)
    both = dot("ps,pr->sr", own, factors.reshape(-1, 2 * rank))
    logits = jnp.sum(own.astype(full) * direct.reshape(-1, 1), axis=0)
    logits = logits + jnp.sum(both[:, :rank] * both[:, rank:], axis=1)
    grad = jax.nn.sigmoid(logits) - labels.astype(full)
    tail = jnp.zeros((samples, 128), full).at[:, 0].set(grad)
    scaled = jnp.concatenate([both * grad[:, None], tail], axis=1).astype(half)
    scaled = lax.all_gather(scaled, "q", axis=0, tiled=True)
    partial = dot("ps,sr->pr", mine.reshape(-1, q_count * samples), scaled).astype(half)
    partial = partial.reshape(z_count * row_count, rows_local, 2 * rank + 128)
    summed = lax.all_to_all(partial, ("z", "row"), 0, 0, tiled=True)
    summed = jnp.sum(summed.astype(full), axis=0)
    whole = lax.all_gather(summed.astype(half), "row", axis=0, tiled=True)
    start = my_table * embed
    down_own = lax.dynamic_slice_in_dim(cross_down, start, embed, 0)
    up_own = lax.dynamic_slice_in_dim(cross_up, start, embed, 1)
    weight_own = lax.dynamic_slice_in_dim(out_weight, start, embed, 0)
    bias_own = lax.dynamic_slice_in_dim(cross_bias, start, embed, 0)
    left, right, count_sum = summed[:, :rank], summed[:, rank : 2 * rank], summed[:, 2 * rank :][:, :1]
    grad_slab = (
        (1.0 + bias_own) * weight_own * count_sum
        + weight_own * dot("pr,re->pe", left.astype(half), up_own)
        + dot("pr,er->pe", right.astype(half), down_own)
    )
    columns = embed // row_count
    at = lax.axis_index("row") * columns
    slab_table = lax.dynamic_index_in_dim(tables, my_table, 0, False)
    slab_own = lax.dynamic_slice_in_dim(slab_table, at, columns, 1)
    weight_part = lax.dynamic_slice_in_dim(weight_own, at, columns, 0)
    bias_part = lax.dynamic_slice_in_dim(bias_own, at, columns, 0)
    up_part = lax.dynamic_slice_in_dim(up_own, at, columns, 1)
    grad_down = dot("pe,pr->er", slab_own, whole[:, rank : 2 * rank])
    core = dot("pr,pe->re", whole[:, :rank], slab_own)
    total = dot("pe,pr->er", slab_own, whole[:, 2 * rank :])[:, 0]
    grad_bias = weight_part * total
    grad_out = (1.0 + bias_part) * total + jnp.sum(up_part.astype(full) * core, axis=0)
    return (
        grad_slab,
        grad_down.astype(half),
        (core * weight_part).astype(half),
        grad_bias,
        grad_out,
    )


def solution(mesh):
    tbl_count, row_count = mesh.shape["tbl"], mesh.shape["row"]
    q_count = inner_count(tbl_count)
    finer = Mesh(mesh.devices.reshape(tbl_count // q_count, q_count, row_count), ("z", "q", "row"))
    every = ("z", "q", "row")
    placed = (P(every, None), P(None, every), P(), P(), P(), P(), P(every))
    return jax.shard_map(
        local,
        mesh=finer,
        in_specs=placed,
        out_specs=(P(every, None), P(every, None), P(None, every), P(every), P(every)),
        check_vma=False,
    )
```

time: 307 us -> 160 us (0.52)
  the two profiles are of different devices: /device:TPU:25 before, /device:TPU:0 now
where the time goes in v1:
time: 160 us; the launch traced here: 159 us
  waiting for transfers between devices  87.7 us (55%)
  blocking collectives  24.1 us (15%)
  matrix products  15.3 us (10%)
  between operations  14.2 us (9%)
  starting transfers between devices  8.32 us (5%)
  other arithmetic  6.78 us (4%)
  local copies, waits for them, and re-layouts  2.58 us (2%)
    all_to_all x1, waiting for transfers between devices, local(): summed = lax.all_to_all(partial, ('z', 'row'), 0, 0, tiled=True)  29.3 us
    all_gather x1, waiting for transfers between devices, local(): scaled = lax.all_gather(scaled, 'q', axis=0, tiled=True)  26.7 us
    all_gather x1, waiting for transfers between devices, local(): tables = lax.all_gather(slab, ('z', 'q', 'row'), axis=0, tiled=True)  23.2 us
    all_to_all x1, blocking collectives, local(): mine = lax.all_to_all(flipped, ('z', 'row'), 0, 0, tiled=True)  22 us
    all_to_all x1, waiting for transfers between devices, local(): own = lax.all_to_all(mine, 'q', 1, 0, tiled=True)  7.84 us
    all_to_all x1, starting transfers between devices, local(): summed = lax.all_to_all(partial, ('z', 'row'), 0, 0, tiled=True)  4.61 us
    all_to_all x1, starting transfers between devices, local(): own = lax.all_to_all(mine, 'q', 1, 0, tiled=True)  3.68 us
    dot_general x1, matrix products, local(): dot('tpe,ter->tpr', tables, down)  3.37 us
  transfers between devices with their start and end apart: 4, of which 4 were waited for; matrix products, arithmetic and copies ran while one was open for 2% of the time, Pallas kernels for 0%

profile of v1, /device:TPU:0, one launch (start us, length us, event | category | flops | bytes accessed | tf_op | source)
XLA Modules:
  0.0 159.0 jit_solution(14185896591672912395)
XLA Ops:
  7.2 0.7 all-gather.3.cloned.1.call-update
  7.9 1.3 convert_bitcast_fusion
  9.2 0.4 reshape.94
  9.6 0.1 copy.38
  9.7 0.2 reshape.95
  9.9 22.0 %all_to_all.25 = bf16[8,64,512]{2,1,0:T(8,128)(2,1)S(1)} all-to-all(bf16[8,64,512]{2,1,0:T(8,128)(2,1)S(1)} %reshape.95), channel_id=1, replica_groups=mesh['z'=4,'q'=4,'row'=2] {'z','row'}, dimensions={0} | all-to-all | bytes 1048576 | tf_op jit(solution)/shard_map/all_to_all | solution.py:28
  32.1 0.9 copy.27
  33.0 3.7 %all-to-all-start.1 = ((bf16[512,4,128]{2,0,1:T(8,128)(2,1)}), bf16[512,4,128]{2,0,1:T(8,128)(2,1)S(1)}, u32[]{:S(2)}, u32[]{:S(2)}) async-start(bf16[512,4,128]{2,0,1:T(8,128)(2,1)} %copy.27), calls=%async_computation.1 | async-start | bytes 1048576 | tf_op jit(solution)/shard_map/all_to_all | solution.py:30
  36.7 0.6 compare_reduce_fusion
  37.4 7.8 %all-to-all-done.1 = bf16[512,4,128]{2,0,1:T(8,128)(2,1)S(1)} async-done(((bf16[512,4,128]{2,0,1:T(8,128)(2,1)}), bf16[512,4,128]{2,0,1:T(8,128)(2,1)S(1)}, u32[]{:S(2)}, u32[]{:S(2)}) %all-to-all-start.1) | async-done | bytes 524320 | tf_op jit(solution)/shard_map/all_to_all | solution.py:30
  45.3 23.2 %all-gather.3.cloned.1.call-done = bf16[2048,256]{1,0:T(8,128)(2,1)} async-done(((bf16[64,256]{1,0:T(8,128)(2,1)}), bf16[2048,256]{1,0:T(8,128)(2,1)}) %all-gather.3.cloned.1.call-update) | async-done | bytes 1048592 | tf_op jit(solution)/shard_map/all_gather | solution.py:32
  68.4 1.6 fusion.7
  70.0 0.4 multiply_reduce_fusion
  70.4 3.4 %convolution_convert_fusion.1 = bf16[16,128,512]{2,1,0:T(8,128)(2,1)S(1)} fusion(bf16[16,128,256]{2,1,0:T(8,128)(2,1)} %bitcast.52, bf16[16,256,512]{2,1,0:T(8,128)(2,1)} %bitcast.57), kind=kOutput, calls=%fused_computation.13 | convolution fusion | flops 537919488 | bytes 7340032 | tf_op jit(solution)/shard_map/tpe,ter->tpr/dot_general | solution.py:38
  73.8 0.7 copy-done.1
  74.4 1.5 fusion.8
  76.0 1.3 fusion.11
  77.4 0.7 fusion.39
  78.1 0.7 fusion.17
  78.9 26.7 %all-gather.5.cloned.1.call-done = bf16[512,1152]{0,1:T(8,128)(2,1)} async-done(((bf16[128,1152]{0,1:T(8,128)(2,1)}), bf16[512,1152]{0,1:T(8,128)(2,1)}) %all-gather.5.cloned.1.call-update) | async-done | bytes 1179664 | tf_op jit(solution)/shard_map/all_gather | solution.py:49
  105.6 3.2 %convolution_convert_fusion = bf16[1152,512]{0,1:T(8,128)(2,1)} fusion(bf16[512,1152]{0,1:T(8,128)(2,1)} %all-gather.5.cloned.1.call-done, bf16[512,512]{1,0:T(8,128)(2,1)S(1)} %bitcast.63), kind=kOutput, calls=%fused_computation.7 | convolution fusion | flops 604569600 | bytes 2883584 | tf_op jit(solution)/shard_map/ps,sr->pr/dot_general | solution.py:50
  108.8 4.6 %all-to-all-start.2 = ((bf16[8,64,1152]{2,1,0:T(8,128)(2,1)}), bf16[8,64,1152]{2,1,0:T(8,128)(2,1)S(1)}, u32[]{:S(2)}, u32[]{:S(2)}) async-start(bf16[8,64,1152]{2,1,0:T(8,128)(2,1)} %bitcast.20), calls=%async_computation.2 | async-start | bytes 2359296 | tf_op jit(solution)/shard_map/all_to_all | solution.py:52
  113.4 29.3 %all-to-all-done.2 = bf16[8,64,1152]{2,1,0:T(8,128)(2,1)S(1)} async-done(((bf16[8,64,1152]{2,1,0:T(8,128)(2,1)}), bf16[8,64,1152]{2,1,0:T(8,128)(2,1)S(1)}, u32[]{:S(2)}, u32[]{:S(2)}) %all-to-all-start.2) | async-done | bytes 1179680 | tf_op jit(solution)/shard_map/all_to_all | solution.py:52
  142.8 0.2 convert_reduce_fusion
  143.1 2.0 %all_gather.11 = bf16[128,1152]{1,0:T(8,128)(2,1)S(1)} all-gather(bf16[64,1152]{1,0:T(8,128)(2,1)S(1)} %convert.25), channel_id=1, replica_groups=mesh['z'=4,'q'=4,'row'=2] {'row'}, dimensions={0}, use_global_device_ids=true | all-gather | bytes 442368 | tf_op jit(solution)/shard_map/all_gather | solution.py:54
  145.1 0.9 convolution_convert_fusion.2
  146.0 0.2 convolution_bitcast_fusion
  146.2 1.1 fusion.14
  147.4 1.8 %convolution_add_fusion = f32[64,256]{1,0:T(8,128)} fusion(f32[64,256]{1,0:T(8,128)S(1)} %fusion.14, bf16[4096,512]{1,0:T(8,128)(2,1)} %param.11, s32[]{:T(128)S(6)} %select_n.22, bf16[64,1152]{1,0:T(8,128)(2,1)S(1)} %convert.25), kind=kOutput, calls=%fused_computation.16 | convolution fusion | flops 16793600 | bytes 458756 | tf_op jit(solution)/shard_map/pr,er->pe/dot_general | solution.py:64
  149.1 0.6 fusion.41
  149.7 1.9 %multiply_reduce_fusion.1 = (f32[128]{0:T(128)S(1)}, bf16[512,128]{1,0:T(8,128)(2,1)}) fusion(bf16[512,4096]{1,0:T(8,128)(2,1)} %param.12, s32[]{:T(128)S(6)} %dynamic_slice.37, f32[128]{0:T(128)S(1)} %get-tuple-element.18, bf16[16,128,256]{2,1,0:T(8,128)(2,1)S(1)} %bitcast.56, s32[]{:T(128)S(6)} %select_n.24, s32[]{:T(128)S(6)} %select_n.26, ...), kind=kOutput, calls=%fused_computation.30 | convolution fusion | flops 17104768 | bytes 427020 | tf_op jit(solution)/shard_map/pr,pe->re/dot_general | solution.py:74
  151.6 0.6 multiply_add_fusion
  (23 shorter events, 0.6 us)
Async XLA Ops:
  7.2 61.3 %all-gather.3.cloned.1.call-start = ((), (), s32[]{:S(2)}) async-start(), calls=%async_computation.3 | async-start | bytes 1081344 | tf_op jit(solution)/shard_map/all_gather | solution.py:32
  9.7 27.0 %copy-start.2 = (f32[4096]{0:T(1024)S(1)}, f32[4096]{0:T(1024)}, u32[]{:S(2)}) copy-start(f32[4096]{0:T(1024)} %param.14) | copy-start | bytes 49156
  9.9 26.8 %copy-start.3 = (f32[4096]{0:T(1024)S(1)}, f32[4096]{0:T(1024)}, u32[]{:S(2)}) copy-start(f32[4096]{0:T(1024)} %param.13) | copy-start | bytes 49156
  33.0 12.2 %all-to-all-start.1 = ((bf16[512,4,128]{2,0,1:T(8,128)(2,1)}), bf16[512,4,128]{2,0,1:T(8,128)(2,1)S(1)}, u32[]{:S(2)}, u32[]{:S(2)}) async-start(bf16[512,4,128]{2,0,1:T(8,128)(2,1)} %copy.27), calls=%async_computation.1 | async-start | bytes 1048576 | tf_op jit(solution)/shard_map/all_to_all | solution.py:30
  36.7 68.9 %all-gather.5.cloned.1.call-start = ((), (), s32[]{:S(2)}) async-start(), calls=%async_computation.4 | async-start | bytes 1474560 | tf_op jit(solution)/shard_map/all_gather | solution.py:49
  70.4 3.4 %copy-start = (bf16[2048,256]{1,0:T(8,128)(2,1)S(1)}, bf16[2048,256]{1,0:T(8,128)(2,1)}, u32[]{:S(2)}) copy-start(bf16[2048,256]{1,0:T(8,128)(2,1)} %all-gather.3.cloned.1.call-done) | copy-start | bytes 3145732
  70.4 4.1 %copy-start.1 = (bf16[512,4096]{1,0:T(8,128)(2,1)S(1)}, bf16[512,4096]{1,0:T(8,128)(2,1)}, u32[]{:S(2)}) copy-start(bf16[512,4096]{1,0:T(8,128)(2,1)} %param.12) | copy-start | bytes 12582916
  76.0 1.4 copy-start.4
  108.8 34.0 %all-to-all-start.2 = ((bf16[8,64,1152]{2,1,0:T(8,128)(2,1)}), bf16[8,64,1152]{2,1,0:T(8,128)(2,1)S(1)}, u32[]{:S(2)}, u32[]{:S(2)}) async-start(bf16[8,64,1152]{2,1,0:T(8,128)(2,1)} %bitcast.20), calls=%async_computation.2 | async-start | bytes 2359296 | tf_op jit(solution)/shard_map/all_to_all | solution.py:52
Sparse Core Ops, SparseCore 0:
  10.9 57.5 all-gather.2
  79.0 26.5 all-gather.4

commit v2 on v1

v2 whole, which is shorter than its diff:
```python
import functools
import math

import jax
import jax.numpy as jnp
from jax import lax
from jax.experimental import pallas as pl
from jax.experimental.pallas import tpu as pltpu
from jax.sharding import Mesh, PartitionSpec as P


def inner_count(count):
    width = max(1, math.isqrt(count))
    while count % width:
        width -= 1
    return width


def kernel(
    slab, flipped, down_hbm, up_hbm, bias, weight, labels,
    sum_out, whole_out, slab_out,
    down, up, send_counts, mine, own, slabs, factors, scaled, part_send, parts, whole,
    load_sem, count_send, count_recv, own_send, own_recv,
    slab_z_send, slab_z_recv, slab_q_send, slab_q_recv, slab_r_send, slab_r_recv,
    scaled_send, scaled_recv, part_send_sem, part_recv_sem, whole_send, whole_recv,
):
    z_count, q_count, row_count = (lax.axis_size(name) for name in ("z", "q", "row"))
    z, q, c = (lax.axis_index(name) for name in ("z", "q", "row"))
    rows, embed = slab.shape
    samples = labels.shape[0]
    rank = down.shape[1]
    half, full = jnp.bfloat16, jnp.float32
    group = z * row_count + c

    def device(at_z, at_q, at_c):
        return (at_z, at_q, at_c)

    def remote(source, target, send, recv, to):
        return pltpu.make_async_remote_copy(
            src_ref=source, dst_ref=target, send_sem=send, recv_sem=recv,
            device_id=to, device_id_type=pl.DeviceIdType.MESH,
        )

    z_peers = [lax.rem(z + step, z_count) for step in range(1, z_count)]
    q_peers = [lax.rem(q + step, q_count) for step in range(1, q_count)]
    c_peers = [lax.rem(c + step, row_count) for step in range(1, row_count)]
    group_peers = [(z, at_c) for at_c in c_peers]
    for at_z in z_peers:
        group_peers += [(at_z, at_c) for at_c in [c] + c_peers]

    loads = [
        pltpu.make_async_copy(down_hbm, down, load_sem.at[0]),
        pltpu.make_async_copy(up_hbm, up, load_sem.at[1]),
    ]
    for load in loads:
        load.start()
    barrier = pltpu.get_barrier_semaphore()
    for at_z, at_c in group_peers:
        pl.semaphore_signal(barrier, inc=1, device_id=device(at_z, q, at_c), device_id_type=pl.DeviceIdType.MESH)
    for at_q in q_peers:
        pl.semaphore_signal(barrier, inc=1, device_id=device(z, at_q, c), device_id_type=pl.DeviceIdType.MESH)
    slabs[q, z, c] = slab[...]

    def fill(at_z, at_c):
        for at_q in range(q_count):
            start = pl.multiple_of(((at_z * q_count + at_q) * row_count + at_c) * samples, 128)
            block = flipped[:, pl.ds(start, samples)].astype(half)
            if at_z is z and at_c is c:
                mine[group, :, at_q * samples : (at_q + 1) * samples] = block
            else:
                send_counts[at_z * row_count + at_c, :, at_q * samples : (at_q + 1) * samples] = block

    for at_z, at_c in group_peers:
        fill(at_z, at_c)
    pl.semaphore_wait(barrier, len(group_peers) + len(q_peers))

    sends = []
    for at_z in z_peers:
        sends.append(remote(slabs.at[q, z, c], slabs.at[q, z, c], slab_z_send.at[at_z], slab_z_recv.at[z], device(at_z, q, c)))
        sends[-1].start()
    for at_z, at_c in group_peers:
        to = at_z * row_count + at_c
        sends.append(remote(send_counts.at[to], mine.at[group], count_send.at[to], count_recv.at[group], device(at_z, q, at_c)))
        sends[-1].start()
    fill(z, c)

    def forward_counts(index):
        for at_q in q_peers:
            block = mine.at[index, :, pl.ds(pl.multiple_of(at_q * samples, 128), samples)]
            remote(block, own.at[q, index], own_send.at[at_q], own_recv.at[q], device(z, at_q, c)).start()

    forward_counts(group)
    for at_z in z_peers:
        remote(slabs.at[q, at_z, c], slabs.at[q, at_z, c], slab_z_send.at[at_z], slab_z_recv.at[at_z], device(at_z, q, c)).wait_recv()
    for at_q in q_peers:
        sends.append(remote(slabs.at[q, :, c], slabs.at[q, :, c], slab_q_send.at[at_q], slab_q_recv.at[q], device(z, at_q, c)))
        sends[-1].start()
    for at_c in c_peers:
        remote(slabs.at[q, :, c], slabs.at[q, :, c], slab_r_send.at[at_c], slab_r_recv.at[c], device(z, q, at_c)).start()
    for at_q in q_peers:
        remote(slabs.at[at_q, :, c], slabs.at[at_q, :, c], slab_q_send.at[at_q], slab_q_recv.at[at_q], device(z, at_q, c)).wait_recv()
        for at_c in c_peers:
            remote(slabs.at[at_q, :, c], slabs.at[at_q, :, c], slab_r_send.at[at_c], slab_r_recv.at[c], device(z, q, at_c)).start()
    for at_c in c_peers:
        remote(slabs.at[:, :, at_c], slabs.at[:, :, at_c], slab_r_send.at[at_c], slab_r_recv.at[at_c], device(z, q, at_c)).wait_recv()

    for at_z, at_c in group_peers:
        index = at_z * row_count + at_c
        remote(mine.at[index], mine.at[index], count_send.at[index], count_recv.at[index], device(at_z, q, at_c)).wait_recv()
        forward_counts(index)

    for load in loads:
        load.wait()

    def one_table(table, carry):
        at = pl.multiple_of(table * embed, 128)
        at_z, at_q = table // q_count, lax.rem(table, q_count)
        block = slabs[at_q, at_z].reshape(row_count * rows, embed)
        wide = block.astype(full)
        heavy = weight[:, pl.ds(at, embed)]
        factors[at_q, at_z, :, :rank] = jnp.dot(block, down[pl.ds(at, embed), :], preferred_element_type=full).astype(half)
        factors[at_q, at_z, :, rank : 2 * rank] = lax.dot_general(
            (wide * heavy).astype(half), up[:, pl.ds(at, embed)], (((1,), (1,)), ((), ())), preferred_element_type=full
        ).astype(half)
        direct = jnp.sum(wide * (heavy * (1.0 + bias[:, pl.ds(at, embed)])), axis=1, keepdims=True)
        upper = direct.astype(half).astype(full)
        lane = lax.broadcasted_iota(jnp.int32, (row_count * rows, 128), 1)
        both = jnp.where(lane == 0, upper, jnp.where(lane == 1, direct - upper, 0.0))
        factors[at_q, at_z, :, 2 * rank :] = both.astype(half)
        return carry

    lax.fori_loop(0, z_count * q_count, one_table, 0)

    own[q] = mine[:, :, pl.ds(pl.multiple_of(q * samples, 128), samples)]
    total = None
    for at_q in [q] + q_peers:
        if at_q is not q:
            remote(own.at[at_q], own.at[at_q], own_send.at[at_q], own_recv.at[at_q], device(z, at_q, c)).wait_recv()
        term = lax.dot_general(
            own[at_q].reshape(z_count * row_count * rows, samples),
            factors[at_q].reshape(z_count * row_count * rows, 2 * rank + 128),
            (((0,), (0,)), ((), ())), preferred_element_type=full,
        )
        total = term if total is None else total + term
    logits = jnp.sum(total[:, 2 * rank :], axis=1, keepdims=True)
    logits = logits + jnp.sum(total[:, :rank] * total[:, rank : 2 * rank], axis=1, keepdims=True)
    grad = jax.nn.sigmoid(logits) - labels[...].astype(full)
    scaled[q, :, : 2 * rank] = (total[:, : 2 * rank] * grad).astype(half)
    lane = lax.broadcasted_iota(jnp.int32, (samples, 128), 1)
    scaled[q, :, 2 * rank :] = jnp.where(lane == 0, grad, 0.0).astype(half)
    for at_q in q_peers:
        sends.append(remote(scaled.at[q], scaled.at[q], scaled_send.at[at_q], scaled_recv.at[q], device(z, at_q, c)))
        sends[-1].start()
    for at_q in q_peers:
        remote(scaled.at[at_q], scaled.at[at_q], scaled_send.at[at_q], scaled_recv.at[at_q], device(z, at_q, c)).wait_recv()
    gathered = scaled[...].reshape(q_count * samples, 2 * rank + 128)
    for at_z in z_peers + [z]:
        counted = mine[pl.ds(at_z * row_count, row_count)].reshape(row_count * rows, q_count * samples)
        term = jnp.dot(counted, gathered, preferred_element_type=full).astype(half)
        part_send[pl.ds(at_z * row_count, row_count)] = term.reshape(row_count, rows, 2 * rank + 128)
        for at_c in [c] + c_peers:
            if at_z is z and at_c is c:
                continue
            to = at_z * row_count + at_c
            sends.append(remote(part_send.at[to], parts.at[group], part_send_sem.at[to], part_recv_sem.at[group], device(at_z, q, at_c)))
            sends[-1].start()
    summed = part_send[group].astype(full)
    for at_z, at_c in group_peers:
        index = at_z * row_count + at_c
        remote(parts.at[index], parts.at[index], part_send_sem.at[index], part_recv_sem.at[index], device(at_z, q, at_c)).wait_recv()
        summed = summed + parts[index].astype(full)
    whole[c] = summed.astype(half)
    for at_c in c_peers:
        sends.append(remote(whole.at[c], whole.at[c], whole_send.at[at_c], whole_recv.at[c], device(z, q, at_c)))
        sends[-1].start()
    sum_out[...] = summed
    slab_out[...] = slabs[q, z].reshape(row_count * rows, embed)
    for at_c in c_peers:
        remote(whole.at[at_c], whole.at[at_c], whole_send.at[at_c], whole_recv.at[at_c], device(z, q, at_c)).wait_recv()
    whole_out[...] = whole[...].reshape(row_count * rows, 2 * rank + 128)
    for copy in sends:
        copy.wait_send()
    for at_q in q_peers:
        remote(own.at[at_q], own.at[at_q], own_send.at[at_q], own_recv.at[at_q], device(z, at_q, c)).wait_send()
    for at_c in c_peers:
        remote(slabs.at[:, :, at_c], slabs.at[:, :, at_c], slab_r_send.at[at_c], slab_r_recv.at[at_c], device(z, q, at_c)).wait_send()


def local(slab, counts, cross_down, cross_up, cross_bias, out_weight, labels):
    z_count, q_count, row_count = (lax.axis_size(name) for name in ("z", "q", "row"))
    rows, embed = slab.shape
    samples = labels.shape[0]
    rank, width = cross_down.shape[1], cross_down.shape[0]
    half, full = jnp.bfloat16, jnp.float32
    dot = functools.partial(jnp.einsum, preferred_element_type=full)
    groups, table_rows, wide = z_count * row_count, row_count * rows, 2 * rank + 128
    vmem, anywhere = pl.BlockSpec(memory_space=pltpu.VMEM), pl.BlockSpec(memory_space=pl.ANY)
    sem = pltpu.SemaphoreType.DMA
    summed, whole, slab_table = pl.pallas_call(
        kernel,
        out_shape=(
            jax.ShapeDtypeStruct((rows, wide), full),
            jax.ShapeDtypeStruct((table_rows, wide), half),
            jax.ShapeDtypeStruct((table_rows, embed), half),
        ),
        in_specs=[vmem, vmem, anywhere, anywhere, vmem, vmem, vmem],
        out_specs=(vmem, vmem, vmem),
        scratch_shapes=[
            pltpu.VMEM((width, rank), half),
            pltpu.VMEM((rank, width), half),
            pltpu.VMEM((groups, rows, q_count * samples), half),
            pltpu.VMEM((groups, rows, q_count * samples), half),
            pltpu.VMEM((q_count, groups, rows, samples), half),
            pltpu.VMEM((q_count, z_count, row_count, rows, embed), half),
            pltpu.VMEM((q_count, z_count, table_rows, wide), half),
            pltpu.VMEM((q_count, samples, wide), half),
            pltpu.VMEM((groups, rows, wide), half),
            pltpu.VMEM((groups, rows, wide), half),
            pltpu.VMEM((row_count, rows, wide), half),
            sem((2,)),
            sem((groups,)), sem((groups,)), sem((q_count,)), sem((q_count,)),
            sem((z_count,)), sem((z_count,)), sem((q_count,)), sem((q_count,)), sem((row_count,)), sem((row_count,)),
            sem((q_count,)), sem((q_count,)), sem((groups,)), sem((groups,)), sem((row_count,)), sem((row_count,)),
        ],
        compiler_params=pltpu.CompilerParams(collective_id=0, has_side_effects=True, vmem_limit_bytes=60 * 2**20),
    )(slab, counts.T, cross_down, cross_up, cross_bias.reshape(1, -1), out_weight.reshape(1, -1), labels.reshape(-1, 1))
    my_table = lax.axis_index("z") * q_count + lax.axis_index("q")
    start = my_table * embed
    down_own = lax.dynamic_slice_in_dim(cross_down, start, embed, 0)
    up_own = lax.dynamic_slice_in_dim(cross_up, start, embed, 1)
    weight_own = lax.dynamic_slice_in_dim(out_weight, start, embed, 0)
    bias_own = lax.dynamic_slice_in_dim(cross_bias, start, embed, 0)
    left, right, count_sum = summed[:, :rank], summed[:, rank : 2 * rank], summed[:, 2 * rank :][:, :1]
    grad_slab = (
        (1.0 + bias_own) * weight_own * count_sum
        + weight_own * dot("pr,re->pe", left.astype(half), up_own)
        + dot("pr,er->pe", right.astype(half), down_own)
    )
    columns = embed // row_count
    at = lax.axis_index("row") * columns
    slab_own = lax.dynamic_slice_in_dim(slab_table, at, columns, 1)
    weight_part = lax.dynamic_slice_in_dim(weight_own, at, columns, 0)
    bias_part = lax.dynamic_slice_in_dim(bias_own, at, columns, 0)
    up_part = lax.dynamic_slice_in_dim(up_own, at, columns, 1)
    grad_down = dot("pe,pr->er", slab_own, whole[:, rank : 2 * rank])
    core = dot("pr,pe->re", whole[:, :rank], slab_own)
    total = dot("pe,pr->er", slab_own, whole[:, 2 * rank :])[:, 0]
    grad_bias = weight_part * total
    grad_out = (1.0 + bias_part) * total + jnp.sum(up_part.astype(full) * core, axis=0)
    return (
        grad_slab,
        grad_down.astype(half),
        (core * weight_part).astype(half),
        grad_bias,
        grad_out,
    )


def solution(mesh):
    tbl_count, row_count = mesh.shape["tbl"], mesh.shape["row"]
    q_count = inner_count(tbl_count)
    finer = Mesh(mesh.devices.reshape(tbl_count // q_count, q_count, row_count), ("z", "q", "row"))
    every = ("z", "q", "row")
    placed = (P(every, None), P(None, every), P(), P(), P(), P(), P(every))
    return jax.shard_map(
        local,
        mesh=finer,
        in_specs=placed,
        out_specs=(P(every, None), P(every, None), P(None, every), P(every), P(every)),
        check_vma=False,
    )
```

time: 160 us -> 91.1 us (0.57)
  the two profiles are of different devices: /device:TPU:0 before, /device:TPU:25 now
where the time goes in v2:
time: 91.1 us; the launch traced here: 90.6 us
  Pallas kernels  75.8 us (83%)
  matrix products  7.58 us (8%)
  other arithmetic  4.33 us (5%)
  local copies, waits for them, and re-layouts  2.25 us (2%)
    pallas_call x1, Pallas kernels, local(): pl.pallas_call(kernel, out_shape=(jax.ShapeDtypeStruct((rows, wide), full...  75.8 us
    dot_general x1, matrix products, local(): core = dot('pr,pe->re', whole[:, :rank], slab_own)  1.93 us

profile of v2, /device:TPU:25, one launch (start us, length us, event | category | flops | bytes accessed | tf_op | source)
XLA Modules:
  0.0 90.6 jit_solution(9348239092722981115)
XLA Ops:
  0.6 1.4 %copy.13.labels = s32[128,1]{1,0:T(8,128)} copy(s32[128,1]{0,1:T(1,128)} %bitcast.9) | data formatting | bytes 1024 | tf_op jit(solution)/shard_map/reshape | solution.py:226
  2.0 75.8 %shard_map.110 = (f32[64,1152]{1,0:T(8,128)}, bf16[128,1152]{1,0:T(8,128)(2,1)}, bf16[128,256]{1,0:T(8,128)(2,1)}) custom-call(bf16[64,256]{1,0:T(8,128)(2,1)} %slab.1, s32[64,4096]{1,0:T(8,128)} %bitcast.6, bf16[4096,512]{1,0:T(8,128)(2,1)} %down_hbm.1, bf16[512,4096]{1,0:T(8,128)(2,1)} %up_hbm.1, f32[1,4096]{1,0:T(1,128)} %bitcast.8, f32[1,4096]{1,0:T(1,128)} %bitcast.7, ...), custom_call_target="tpu_custom_call" | custom-call | tf_op jit(solution)/shard_map/pallas_call | solution.py:199
  77.8 1.0 %convert.4 = bf16[64,1152]{1,0:T(8,128)(2,1)S(1)} convert(f32[64,1152]{1,0:T(8,128)} %get-tuple-element.8) | non-fusion elementwise | flops 73728 | bytes 442368 | tf_op jit(solution)/shard_map/convert.1
  78.8 0.8 add_multiply_fusion
  79.6 0.9 slice_reduce_fusion
  80.4 1.1 %fusion = f32[64,256]{1,0:T(8,128)S(1)} fusion(bf16[512,4096]{1,0:T(8,128)(2,1)} %up_hbm.1, s32[]{:T(128)S(6)} %select_n.16, bf16[64,1152]{1,0:T(8,128)(2,1)S(1)} %convert.4, f32[256]{0:T(256)S(1)} %get-tuple-element.14, f32[64]{0:T(128)S(1)} %slice_reduce_fusion, f32[256]{0:T(256)S(1)} %get-tuple-element.13), kind=kOutput, calls=%fused_computation.3 | convolution fusion | flops 16826368 | bytes 395780 | tf_op jit(solution)/shard_map/pr,re->pe/dot_general | solution.py:236
  81.6 1.8 %convolution_add_fusion = f32[64,256]{1,0:T(8,128)} fusion(f32[64,256]{1,0:T(8,128)S(1)} %fusion, bf16[4096,512]{1,0:T(8,128)(2,1)} %down_hbm.1, s32[]{:T(128)S(6)} %select_n.16, bf16[64,1152]{1,0:T(8,128)(2,1)S(1)} %convert.4), kind=kOutput, calls=%fused_computation.1 | convolution fusion | flops 16793600 | bytes 458756 | tf_op jit(solution)/shard_map/pr,er->pe/dot_general | solution.py:237
  83.4 1.8 %convolution_convert_fusion = bf16[128,512]{1,0:T(8,128)(2,1)} fusion(bf16[128,1152]{1,0:T(8,128)(2,1)} %get-tuple-element.10, bf16[128,256]{1,0:T(8,128)(2,1)} %get-tuple-element.9, s32[]{:T(128)S(6)} %select_n.17), kind=kOutput, calls=%fused_computation | convolution fusion | flops 16842752 | bytes 294916 | tf_op jit(solution)/shard_map/pe,pr->er/dot_general | solution.py:245
  85.2 0.9 %convolution_bitcast_fusion = f32[128]{0:T(128)S(1)} fusion(bf16[128,1152]{1,0:T(8,128)(2,1)} %get-tuple-element.10, bf16[128,256]{1,0:T(8,128)(2,1)} %get-tuple-element.9, s32[]{:T(128)S(6)} %select_n.17), kind=kOutput, calls=%fused_computation.4 | convolution fusion | flops 32768 | bytes 66052 | tf_op jit(solution)/shard_map/pe,pr->er/dot_general | solution.py:247
  86.1 1.3 %fusion.17 = (f32[128]{0:T(128)}, f32[128]{0:T(128)S(1)}) fusion(f32[128]{0:T(128)S(1)} %convolution_bitcast_fusion, f32[4096]{0:T(1024)} %param.12, s32[]{:T(128)S(6)} %dynamic_slice.32), kind=kLoop, calls=%fused_computation.26 | loop fusion | flops 128 | bytes 2052 | tf_op jit(solution)/shard_map/mul | solution.py:248
  87.4 1.9 %multiply_reduce_fusion = (f32[128]{0:T(128)S(1)}, bf16[512,128]{1,0:T(8,128)(2,1)}) fusion(bf16[512,4096]{1,0:T(8,128)(2,1)} %up_hbm.1, s32[]{:T(128)S(6)} %dynamic_slice.32, f32[128]{0:T(128)S(1)} %get-tuple-element.12, bf16[128,256]{1,0:T(8,128)(2,1)} %get-tuple-element.9, s32[]{:T(128)S(6)} %select_n.17, bf16[128,1152]{1,0:T(8,128)(2,1)} %get-tuple-element.10), kind=kOutput, calls=%fused_computation.5 | convolution fusion | flops 17104768 | bytes 427016 | tf_op jit(solution)/shard_map/pr,pe->re/dot_general | solution.py:246
  89.3 1.3 %multiply_add_fusion = f32[128]{0:T(128)} fusion(f32[128]{0:T(128)S(1)} %get-tuple-element.15, f32[128]{0:T(128)S(1)} %convolution_bitcast_fusion, f32[4096]{0:T(1024)} %param.11, s32[]{:T(128)S(6)} %dynamic_slice.32), kind=kLoop, calls=%fused_computation.25 | loop fusion | flops 384 | bytes 2052 | tf_op jit(solution)/shard_map/add | solution.py:249

commit v3 on v2

--- a/solution.py
+++ b/solution.py
@@ -17,17 +17,20 @@
 
 
 def kernel(
-    slab, flipped, down_hbm, up_hbm, bias, weight, labels,
-    sum_out, whole_out, slab_out,
+    inside, out_count, slab, flipped, down_hbm, up_hbm, bias, weight, labels,
+    *refs,
+):
+    outs, rest = refs[:out_count], refs[out_count:]
+    (
     down, up, send_counts, mine, own, slabs, factors, scaled, part_send, parts, whole,
     load_sem, count_send, count_recv, own_send, own_recv,
     slab_z_send, slab_z_recv, slab_q_send, slab_q_recv, slab_r_send, slab_r_recv,
     scaled_send, scaled_recv, part_send_sem, part_recv_sem, whole_send, whole_recv,
-):
+    ) = rest
     z_count, q_count, row_count = (lax.axis_size(name) for name in ("z", "q", "row"))
     z, q, c = (lax.axis_index(name) for name in ("z", "q", "row"))
     rows, embed = slab.shape
-    samples = labels.shape[0]
+    samples = labels.shape[1]
     rank = down.shape[1]
     half, full = jnp.bfloat16, jnp.float32
     group = z * row_count + c
@@ -144,40 +147,92 @@
         total = term if total is None else total + term
     logits = jnp.sum(total[:, 2 * rank :], axis=1, keepdims=True)
     logits = logits + jnp.sum(total[:, :rank] * total[:, rank : 2 * rank], axis=1, keepdims=True)
-    grad = jax.nn.sigmoid(logits) - labels[...].astype(full)
+    own_row = lax.broadcasted_iota(jnp.int32, (samples, samples), 0)
+    own_lane = lax.broadcasted_iota(jnp.int32, (samples, samples), 1)
+    clicked = jnp.sum(jnp.where(own_row == own_lane, labels[...].astype(full), 0.0), axis=1, keepdims=True)
+    grad = jax.nn.sigmoid(logits) - clicked
     scaled[q, :, : 2 * rank] = (total[:, : 2 * rank] * grad).astype(half)
     lane = lax.broadcasted_iota(jnp.int32, (samples, 128), 1)
     scaled[q, :, 2 * rank :] = jnp.where(lane == 0, grad, 0.0).astype(half)
-    for at_q in q_peers:
-        sends.append(remote(scaled.at[q], scaled.at[q], scaled_send.at[at_q], scaled_recv.at[q], device(z, at_q, c)))
-        sends[-1].start()
-    for at_q in q_peers:
-        remote(scaled.at[at_q], scaled.at[at_q], scaled_send.at[at_q], scaled_recv.at[at_q], device(z, at_q, c)).wait_recv()
-    gathered = scaled[...].reshape(q_count * samples, 2 * rank + 128)
-    for at_z in z_peers + [z]:
-        counted = mine[pl.ds(at_z * row_count, row_count)].reshape(row_count * rows, q_count * samples)
-        term = jnp.dot(counted, gathered, preferred_element_type=full).astype(half)
-        part_send[pl.ds(at_z * row_count, row_count)] = term.reshape(row_count, rows, 2 * rank + 128)
-        for at_c in [c] + c_peers:
-            if at_z is z and at_c is c:
-                continue
-            to = at_z * row_count + at_c
-            sends.append(remote(part_send.at[to], parts.at[group], part_send_sem.at[to], part_recv_sem.at[group], device(at_z, q, at_c)))
+    spans = (pl.ds(0, rank), pl.ds(rank, rank + 128))
+    for turn, span in enumerate(spans):
+        for at_q in q_peers:
+            sends.append(remote(
+                scaled.at[q, :, span], scaled.at[q, :, span],
+                scaled_send.at[turn, at_q], scaled_recv.at[turn, q], device(z, at_q, c),
+            ))
             sends[-1].start()
-    summed = part_send[group].astype(full)
-    for at_z, at_c in group_peers:
-        index = at_z * row_count + at_c
-        remote(parts.at[index], parts.at[index], part_send_sem.at[index], part_recv_sem.at[index], device(at_z, q, at_c)).wait_recv()
-        summed = summed + parts[index].astype(full)
+    for turn, span in enumerate(spans):
+        for at_q in q_peers:
+            remote(
+                scaled.at[at_q, :, span], scaled.at[at_q, :, span],
+                scaled_send.at[turn, at_q], scaled_recv.at[turn, at_q], device(z, at_q, c),
+            ).wait_recv()
+        gathered = scaled[:, :, span].reshape(q_count * samples, span.size)
+        for at_z in z_peers + [z]:
+            counted = mine[pl.ds(at_z * row_count, row_count)].reshape(row_count * rows, q_count * samples)
+            term = jnp.dot(counted, gathered, preferred_element_type=full).astype(half)
+            part_send[pl.ds(at_z * row_count, row_count), :, span] = term.reshape(row_count, rows, span.size)
+            for at_c in [c] + c_peers:
+                if at_z is z and at_c is c:
+                    continue
+                to = at_z * row_count + at_c
+                sends.append(remote(
+                    part_send.at[to, :, span], parts.at[group, :, span],
+                    part_send_sem.at[turn, to], part_recv_sem.at[turn, group], device(at_z, q, at_c),
+                ))
+                sends[-1].start()
+    sums = []
+    for turn, span in enumerate(spans):
+        summed = part_send[group, :, span].astype(full)
+        for at_z, at_c in group_peers:
+            index = at_z * row_count + at_c
+            remote(
+                parts.at[index, :, span], parts.at[index, :, span],
+                part_send_sem.at[turn, index], part_recv_sem.at[turn, index], device(at_z, q, at_c),
+            ).wait_recv()
+            summed = summed + parts[index, :, span].astype(full)
+        sums.append(summed)
+    summed = jnp.concatenate(sums, axis=1)
     whole[c] = summed.astype(half)
     for at_c in c_peers:
         sends.append(remote(whole.at[c], whole.at[c], whole_send.at[at_c], whole_recv.at[c], device(z, q, at_c)))
         sends[-1].start()
-    sum_out[...] = summed
-    slab_out[...] = slabs[q, z].reshape(row_count * rows, embed)
+    if inside:
+        slab_grad, down_grad, up_grad, bias_grad, out_grad = outs
+        at = pl.multiple_of((z * q_count + q) * embed, 128)
+        heavy, raised = weight[:, pl.ds(at, embed)], 1.0 + bias[:, pl.ds(at, embed)]
+        back = jnp.dot(summed[:, :rank].astype(half), up[:, pl.ds(at, embed)], preferred_element_type=full)
+        slab_grad[...] = (
+            raised * heavy * summed[:, 2 * rank : 2 * rank + 1]
+            + heavy * back
+            + lax.dot_general(
+                summed[:, rank : 2 * rank].astype(half), down[pl.ds(at, embed), :],
+                (((1,), (1,)), ((), ())), preferred_element_type=full,
+            )
+        )
+    else:
+        sum_out, whole_out, slab_out = outs
+        sum_out[...] = summed
+        slab_out[...] = slabs[q, z].reshape(row_count * rows, embed)
     for at_c in c_peers:
         remote(whole.at[at_c], whole.at[at_c], whole_send.at[at_c], whole_recv.at[at_c], device(z, q, at_c)).wait_recv()
-    whole_out[...] = whole[...].reshape(row_count * rows, 2 * rank + 128)
+    everything = whole[...].reshape(row_count * rows, 2 * rank + 128)
+    if inside:
+        columns = embed // row_count
+        place = pl.multiple_of(c * columns, 128)
+        mixed = slabs[q, z, :, :, pl.ds(place, columns)].reshape(row_count * rows, columns)
+        first = (((0,), (0,)), ((), ()))
+        at = pl.multiple_of((z * q_count + q) * embed + c * columns, 128)
+        heavy, raised = weight[:, pl.ds(at, columns)], 1.0 + bias[:, pl.ds(at, columns)]
+        down_grad[...] = lax.dot_general(mixed, everything[:, rank : 2 * rank], first, preferred_element_type=full).astype(half)
+        core = lax.dot_general(everything[:, :rank], mixed, first, preferred_element_type=full)
+        up_grad[...] = (core * heavy).astype(half)
+        counted = lax.dot_general(everything[:, 2 * rank :], mixed, first, preferred_element_type=full)[:1]
+        bias_grad[...] = heavy * counted
+        out_grad[...] = raised * counted + jnp.sum(up[:, pl.ds(at, columns)].astype(full) * core, axis=0, keepdims=True)
+    else:
+        whole_out[...] = everything
     for copy in sends:
         copy.wait_send()
     for at_q in q_peers:
@@ -196,15 +251,27 @@
     groups, table_rows, wide = z_count * row_count, row_count * rows, 2 * rank + 128
     vmem, anywhere = pl.BlockSpec(memory_space=pltpu.VMEM), pl.BlockSpec(memory_space=pl.ANY)
     sem = pltpu.SemaphoreType.DMA
-    summed, whole, slab_table = pl.pallas_call(
-        kernel,
-        out_shape=(
+    columns = embed // row_count
+    inside = columns % 128 == 0
+    if inside:
+        shapes = (
+            jax.ShapeDtypeStruct((rows, embed), full),
+            jax.ShapeDtypeStruct((columns, rank), half),
+            jax.ShapeDtypeStruct((rank, columns), half),
+            jax.ShapeDtypeStruct((1, columns), full),
+            jax.ShapeDtypeStruct((1, columns), full),
+        )
+    else:
+        shapes = (
             jax.ShapeDtypeStruct((rows, wide), full),
             jax.ShapeDtypeStruct((table_rows, wide), half),
             jax.ShapeDtypeStruct((table_rows, embed), half),
-        ),
+        )
+    results = pl.pallas_call(
+        functools.partial(kernel, inside, len(shapes)),
+        out_shape=shapes,
         in_specs=[vmem, vmem, anywhere, anywhere, vmem, vmem, vmem],
-        out_specs=(vmem, vmem, vmem),
+        out_specs=(vmem,) * len(shapes),
         scratch_shapes=[
             pltpu.VMEM((width, rank), half),
             pltpu.VMEM((rank, width), half),
@@ -220,10 +287,14 @@
             sem((2,)),
             sem((groups,)), sem((groups,)), sem((q_count,)), sem((q_count,)),
             sem((z_count,)), sem((z_count,)), sem((q_count,)), sem((q_count,)), sem((row_count,)), sem((row_count,)),
-            sem((q_count,)), sem((q_count,)), sem((groups,)), sem((groups,)), sem((row_count,)), sem((row_count,)),
+            sem((2, q_count)), sem((2, q_count)), sem((2, groups)), sem((2, groups)), sem((row_count,)), sem((row_count,)),
         ],
         compiler_params=pltpu.CompilerParams(collective_id=0, has_side_effects=True, vmem_limit_bytes=60 * 2**20),
-    )(slab, counts.T, cross_down, cross_up, cross_bias.reshape(1, -1), out_weight.reshape(1, -1), labels.reshape(-1, 1))
+    )(slab, counts.T, cross_down, cross_up, cross_bias.reshape(1, -1), out_weight.reshape(1, -1), labels.reshape(1, -1))
+    if inside:
+        slab_grad, down_grad, up_grad, bias_grad, out_grad = results
+        return slab_grad, down_grad, up_grad, bias_grad.reshape(-1), out_grad.reshape(-1)
+    summed, whole, slab_table = results
     my_table = lax.axis_index("z") * q_count + lax.axis_index("q")
     start = my_table * embed
     down_own = lax.dynamic_slice_in_dim(cross_down, start, embed, 0)

time: 91.1 us -> 76.9 us (0.84)
  matrix products: 7.58 us -> 0 us
  Pallas kernels: 75.8 us -> 69.1 us
  local copies, waits for them, and re-layouts: 2.25 us -> 6.84 us
  other arithmetic: 4.33 us -> 0 us
    dot_general x5 -> x0, matrix products: 7.58 us -> none  [the longest x1 1.93 us: local(): core = dot('pr,pe->re', whole[:, :rank], slab_own)]
    unnamed x0 -> x5, local copies, waits for them, and re-layouts: none -> 6.84 us
    pallas_call x1, Pallas kernels: 75.8 us -> 69.1 us  [local(): pl.pallas_call(functools.partial(kernel, inside, len(shapes)), out_shape=...]
    mul x2 -> x0, other arithmetic: 2.07 us -> none  [the longest x1 1.29 us: local(): grad_bias = weight_part * total]
    reshape x1 -> x0, local copies, waits for them, and re-layouts: 1.39 us -> none  [local(): labels.reshape(-1, 1)]
    add x1 -> x0, other arithmetic: 1.27 us -> none  [local(): (1.0 + bias_part) * total + jnp.sum(up_part.astype(full) * core, axis=0)]
    another operation x1 -> x0, other arithmetic: 0.98 us -> none
where the time goes in v3:
time: 76.9 us; the launch traced here: 76.6 us
  Pallas kernels  69.1 us (90%)
  local copies, waits for them, and re-layouts  6.84 us (9%)
    pallas_call x1, Pallas kernels, local(): pl.pallas_call(functools.partial(kernel, inside, len(shapes)), out_shape=...  69.1 us
    unnamed x5, local copies, waits for them, and re-layouts  6.84 us

profile of v3, /device:TPU:25, one launch (start us, length us, event | category | flops | bytes accessed | tf_op | source)
XLA Modules:
  0.0 76.6 jit_solution(4670218093297342155)
XLA Ops:
  0.6 69.1 %shard_map.110 = (f32[64,256]{1,0:T(8,128)}, bf16[128,512]{1,0:T(8,128)(2,1)}, bf16[512,128]{1,0:T(8,128)(2,1)}, f32[1,128]{1,0:T(1,128)}, f32[1,128]{1,0:T(1,128)}) custom-call(bf16[64,256]{1,0:T(8,128)(2,1)} %slab.1, s32[64,4096]{1,0:T(8,128)} %bitcast.6, bf16[4096,512]{1,0:T(8,128)(2,1)} %down_hbm.1, bf16[512,4096]{1,0:T(8,128)(2,1)} %up_hbm.1, ...), custom_call_target="tpu_custom_call" | custom-call | tf_op jit(solution)/shard_map/pallas_call | solution.py:270
  69.8 1.5 %copy.17 = f32[64,256]{1,0:T(8,128)} copy(f32[64,256]{1,0:T(8,128)} %get-tuple-element.20) | data formatting | bytes 131072
  71.3 1.6 %copy.18 = bf16[128,512]{1,0:T(8,128)(2,1)} copy(bf16[128,512]{1,0:T(8,128)(2,1)} %get-tuple-element.21) | data formatting | bytes 262144
  72.8 1.6 %copy.19 = bf16[512,128]{1,0:T(8,128)(2,1)} copy(bf16[512,128]{1,0:T(8,128)(2,1)} %get-tuple-element.22) | data formatting | bytes 262144
  74.4 1.1 %copy.20 = f32[128]{0:T(128)} copy(f32[128]{0:T(128)} %bitcast.11) | data formatting | bytes 1024
  75.5 1.1 %copy.21 = f32[128]{0:T(128)} copy(f32[128]{0:T(128)} %bitcast.10) | data formatting | bytes 1024

commit v4 on v3

--- a/solution.py
+++ b/solution.py
@@ -92,7 +92,14 @@
             block = mine.at[index, :, pl.ds(pl.multiple_of(at_q * samples, 128), samples)]
             remote(block, own.at[q, index], own_send.at[at_q], own_recv.at[q], device(z, at_q, c)).start()
 
+    def receive_counts(peers):
+        for at_z, at_c in peers:
+            index = at_z * row_count + at_c
+            remote(mine.at[index], mine.at[index], count_send.at[index], count_recv.at[index], device(at_z, q, at_c)).wait_recv()
+            forward_counts(index)
+
     forward_counts(group)
+    receive_counts(group_peers[: row_count - 1])
     for at_z in z_peers:
         remote(slabs.at[q, at_z, c], slabs.at[q, at_z, c], slab_z_send.at[at_z], slab_z_recv.at[at_z], device(at_z, q, c)).wait_recv()
     for at_q in q_peers:
@@ -104,13 +111,10 @@
         remote(slabs.at[at_q, :, c], slabs.at[at_q, :, c], slab_q_send.at[at_q], slab_q_recv.at[at_q], device(z, at_q, c)).wait_recv()
         for at_c in c_peers:
             remote(slabs.at[at_q, :, c], slabs.at[at_q, :, c], slab_r_send.at[at_c], slab_r_recv.at[c], device(z, q, at_c)).start()
+
+    receive_counts(group_peers[row_count - 1 :])
     for at_c in c_peers:
         remote(slabs.at[:, :, at_c], slabs.at[:, :, at_c], slab_r_send.at[at_c], slab_r_recv.at[at_c], device(z, q, at_c)).wait_recv()
-
-    for at_z, at_c in group_peers:
-        index = at_z * row_count + at_c
-        remote(mine.at[index], mine.at[index], count_send.at[index], count_recv.at[index], device(at_z, q, at_c)).wait_recv()
-        forward_counts(index)
 
     for load in loads:
         load.wait()

time: 76.9 us -> 74.9 us (0.974); the launches traced: 76.6 us -> 73.8 us
  Pallas kernels: 69.1 us -> 66.3 us
    pallas_call x1, Pallas kernels: 69.1 us -> 66.3 us  [local(): pl.pallas_call(functools.partial(kernel, inside, len(shapes)), out_shape=...]
where the time goes in v4:
time: 74.9 us; the launch traced here: 73.8 us
  Pallas kernels  66.3 us (89%)
  local copies, waits for them, and re-layouts  6.84 us (9%)
    pallas_call x1, Pallas kernels, local(): pl.pallas_call(functools.partial(kernel, inside, len(shapes)), out_shape=...  66.3 us
    unnamed x5, local copies, waits for them, and re-layouts  6.84 us

profile of v4, /device:TPU:25, one launch (start us, length us, event | category | flops | bytes accessed | tf_op | source)
XLA Modules:
  0.0 73.8 jit_solution(7434478683037817581)
XLA Ops:
  0.6 66.3 %shard_map.110 = (f32[64,256]{1,0:T(8,128)}, bf16[128,512]{1,0:T(8,128)(2,1)}, bf16[512,128]{1,0:T(8,128)(2,1)}, f32[1,128]{1,0:T(1,128)}, f32[1,128]{1,0:T(1,128)}) custom-call(bf16[64,256]{1,0:T(8,128)(2,1)} %slab.1, s32[64,4096]{1,0:T(8,128)} %bitcast.6, bf16[4096,512]{1,0:T(8,128)(2,1)} %down_hbm.1, bf16[512,4096]{1,0:T(8,128)(2,1)} %up_hbm.1, ...), custom_call_target="tpu_custom_call" | custom-call | tf_op jit(solution)/shard_map/pallas_call | solution.py:274
  67.0 1.5 %copy.17 = f32[64,256]{1,0:T(8,128)} copy(f32[64,256]{1,0:T(8,128)} %get-tuple-element.20) | data formatting | bytes 131072
  68.5 1.6 %copy.18 = bf16[128,512]{1,0:T(8,128)(2,1)} copy(bf16[128,512]{1,0:T(8,128)(2,1)} %get-tuple-element.21) | data formatting | bytes 262144
  70.0 1.6 %copy.19 = bf16[512,128]{1,0:T(8,128)(2,1)} copy(bf16[512,128]{1,0:T(8,128)(2,1)} %get-tuple-element.22) | data formatting | bytes 262144
  71.6 1.1 %copy.20 = f32[128]{0:T(128)} copy(f32[128]{0:T(128)} %bitcast.11) | data formatting | bytes 1024
  72.7 1.1 %copy.21 = f32[128]{0:T(128)} copy(f32[128]{0:T(128)} %bitcast.10) | data formatting | bytes 1024
